TPU v7x, 128 devices: a whole 4x4x4 slice. The times are simulated.
128 devices in a mesh: dp: 32 (over z, y, x_hi), expert: 4 (over x_lo, core).
Axes of the slice: x: 4 (x_hi: 2, x_lo: 2; x = x_hi * 2 + x_lo), y: 4, z: 4, core: 2. Of those that a mesh axis runs over, the one named last changes fastest.
Arguments:
- resid: bfloat16 [16384, 2048], P(('dp', 'expert')), may hold values from -6 to 6
- norm_gain: float32 [2048], replicated, may hold values from 0.25 to 1.75
- w_gate: bfloat16 [128, 2048, 768], P(('dp', 'expert')), may hold values from -0.125 to 0.125
- w_up: bfloat16 [128, 2048, 768], P(('dp', 'expert')), may hold values from -0.125 to 0.125
- w_down: bfloat16 [128, 768, 2048], P(('dp', 'expert')), may hold values from -0.21875 to 0.21875
- route_ids: int32 [16384, 8], P(('dp', 'expert')), may hold values from 0 to 127, as said below
- route_slots: int32 [16384, 8], P(('dp', 'expert')), may hold values from -1 to 19, as said below
- route_weights: float32 [16384, 8], P(('dp', 'expert')), may hold values from 0.02 to 0.5
Outputs:
- stream_out: bfloat16 [16384, 2048], P(('dp', 'expert'))
Inputs may be any that keep to these rules, and one draw needn't show every extreme that they name: `route_ids`: each row names 8 different experts. `route_slots`: -1 marks a dropped choice. Among the rows of one device, the kept choices of one expert hold the slots 0, 1, 2, ... without repeats. Three experts, the same for all devices, have slots below 20; all others have slots below 10. On every device each of those three fills all 20 of its slots and some other expert fills all 10.
All inputs are finite; a program needn't handle non-finite values.
Results may differ from a plain program's by a relative error of at most 0.0044.
Values may be sent and summed in bfloat16 or wider, within the bound.
A program may use at most 128 MiB of HBM per device.

v0:
```python
import jax
import jax.numpy as jnp
from jax import lax
from jax.sharding import PartitionSpec as P

ROUTE_FANOUT = 8


epsilon = 1e-06


def place_rows(normed, row_index, row_count):
    tok_rows, choices_count = row_index.shape
    source = jnp.broadcast_to(
        normed[:, None, :], (tok_rows, choices_count, normed.shape[1])
    ).reshape(tok_rows * choices_count, normed.shape[1])
    empty = jnp.zeros((row_count, normed.shape[1]), jnp.bfloat16)
    return empty.at[row_index.reshape(-1)].set(source, mode="drop")


def expert_work(arrived, w_gate, w_up, w_down):
    gate_sum = jnp.einsum("secd,edf->secf", arrived, w_gate, preferred_element_type=jnp.float32)
    up_sum = jnp.einsum("secd,edf->secf", arrived, w_up, preferred_element_type=jnp.float32)
    hidden = (jax.nn.silu(gate_sum) * up_sum).astype(jnp.bfloat16)
    return jnp.einsum("secf,efd->secd", hidden, w_down, preferred_element_type=jnp.float32).astype(
        jnp.bfloat16
    )


def per_device(resid, norm_gain, w_gate, w_up, w_down, route_ids, route_slots, route_weights):
    rows_dp = lax.axis_size("dp")
    rows_expert = lax.axis_size("expert")
    token_groups = rows_dp * rows_expert
    tok_rows, width = resid.shape
    local_experts = w_gate.shape[0]
    total_experts = local_experts * token_groups
    cap_cold = 5 * tok_rows * ROUTE_FANOUT // (4 * total_experts)
    cap_hot = 2 * cap_cold
    floats = resid.astype(jnp.float32)
    mean_square = jnp.mean(floats * floats, axis=1, keepdims=True)
    normed = (floats * lax.rsqrt(mean_square + epsilon) * norm_gain[None, :]).astype(jnp.bfloat16)
    retained = route_slots >= 0
    row_count = total_experts * cap_hot
    row_index = jnp.where(retained, route_ids * cap_hot + route_slots, row_count)
    outgoing = place_rows(normed, row_index, row_count)
    arrived = lax.all_to_all(
        outgoing.reshape(token_groups, local_experts, cap_hot, width),
        ("dp", "expert"),
        split_axis=0,
        concat_axis=0,
        tiled=True,
    )
    results = expert_work(arrived, w_gate, w_up, w_down)
    returned = lax.all_to_all(results, ("dp", "expert"), split_axis=0, concat_axis=0, tiled=True)
    row_table = returned.reshape(row_count, width)
    padded_table = jnp.concatenate([row_table, jnp.zeros((1, width), jnp.bfloat16)], axis=0)
    picked = padded_table[row_index]
    combined = jnp.sum(picked.astype(jnp.float32) * route_weights[:, :, None], axis=1)
    return (floats + combined).astype(jnp.bfloat16)


def solution(mesh):
    placed = (
        P(("dp", "expert"), None),
        P(),
        P(("dp", "expert"), None, None),
        P(("dp", "expert"), None, None),
        P(("dp", "expert"), None, None),
        P(("dp", "expert"), None),
        P(("dp", "expert"), None),
        P(("dp", "expert"), None),
    )
    return jax.shard_map(
        per_device, mesh=mesh, in_specs=placed, out_specs=P(("dp", "expert"), None), check_vma=False
    )
```

profile of v0, /device:TPU:52, one launch (start us, length us, event | category | flops | bytes accessed | tf_op | source)
XLA Modules:
  0.0 486.3 jit_solution(3766046460607029497)
XLA Ops:
  0.0 0.0 copy-start
  0.0 0.9 compare_select_fusion.1
  0.9 0.1 copy.15
  1.0 0.1 reshape.71
  1.1 1.2 fusion.20
  2.3 2.0 fusion.22
  4.3 12.8 %scatter_custom_fusion = bf16[2560,2048]{1,0:T(8,128)(2,1)} fusion(s32[1024]{0:T(1024)S(1)} %bitcast.74, bf16[]{:T(256)} %constant.9.clone.1, bf16[128,2048]{1,0:T(8,128)(2,1)} %fusion.22), kind=kCustom, calls=%fused_computation.18 | custom fusion | bytes 11010050 | tf_op jit(solution)/shard_map/scatter | solution.py:18
  17.2 16.4 %reshape.73 = bf16[128,1,20,2048]{3,2,0,1:T(8,128)(2,1)} reshape(bf16[2560,2048]{1,0:T(8,128)(2,1)} %scatter_custom_fusion) | data formatting | bytes 20971520 | tf_op jit(solution)/shard_map/reshape | solution.py:47
  33.6 0.0 copy-start.4
  33.6 149.4 %all_to_all.10 = bf16[128,1,20,2048]{3,2,1,0:T(8,128)(2,1)S(1)} all-to-all(bf16[128,1,20,2048]{3,2,1,0:T(8,128)(2,1)} %bitcast.73), channel_id=1, replica_groups=mesh['dp'=32,'expert'=4] {'dp','expert'}, dimensions={0} | all-to-all | bytes 20971520 | tf_op jit(solution)/shard_map/all_to_all | solution.py:46
  183.0 0.0 copy-start.2
  183.0 4.5 copy-done.2
  187.5 0.0 copy-done.4
  187.5 21.8 %fusion = f32[128,20,768]{2,0,1:T(8,128)} fusion(bf16[128,1,20,2048]{3,2,1,0:T(8,128)(2,1)S(1)} %all_to_all.10, bf16[1,2048,768]{2,1,0:T(8,128)(2,1)S(1)} %copy-done.4), kind=kOutput, calls=%fused_computation.2 | convolution fusion | flops 8053063680 | bytes 21495808 | tf_op jit(solution)/shard_map/secd,edf->secf/dot_general | solution.py:23
  209.3 0.0 copy-done
  209.3 32.9 %convert_bitcast_fusion = bf16[128,1,20,2048]{3,0,2,1:T(8,128)(2,1)} fusion(f32[128,20,768]{2,0,1:T(8,128)} %fusion, bf16[1,768,2048]{2,1,0:T(8,128)(2,1)S(1)} %copy-done, bf16[128,1,20,2048]{3,2,1,0:T(8,128)(2,1)} %copy-done.2, bf16[1,2048,768]{2,1,0:T(8,128)(2,1)} %param.10), kind=kOutput, calls=%fused_computation.6 | convolution fusion | flops 16123166720 | bytes 35127296 | tf_op jit(solution)/shard_map/secf,efd->secd/dot_general | solution.py:25
  242.2 14.3 %copy.18 = bf16[128,1,20,2048]{3,2,1,0:T(8,128)(2,1)} copy(bf16[128,1,20,2048]{3,0,2,1:T(8,128)(2,1)} %convert_bitcast_fusion) | data formatting | bytes 20971520 | tf_op jit(solution)/shard_map/convert_element_type | solution.py:25
  256.5 0.0 copy-start.3
  256.5 9.9 %all-to-all-start.1 = ((bf16[128,1,20,2048]{3,2,1,0:T(8,128)(2,1)}), bf16[128,1,20,2048]{3,2,1,0:T(8,128)(2,1)}, u32[]{:S(2)}, u32[]{:S(2)}) async-start(bf16[128,1,20,2048]{3,2,1,0:T(8,128)(2,1)} %copy.18), calls=%async_computation.1 | async-start | bytes 25165824 | tf_op jit(solution)/shard_map/all_to_all | solution.py:54
  266.4 0.1 copy.19
  266.5 0.1 reshape.82
  266.6 0.0 copy-done.3
  266.6 0.1 copy.20
  266.7 170.1 %all-to-all-done.1 = bf16[128,1,20,2048]{3,2,1,0:T(8,128)(2,1)} async-done(((bf16[128,1,20,2048]{3,2,1,0:T(8,128)(2,1)}), bf16[128,1,20,2048]{3,2,1,0:T(8,128)(2,1)}, u32[]{:S(2)}, u32[]{:S(2)}) %all-to-all-start.1) | async-done | bytes 10485792 | tf_op jit(solution)/shard_map/all_to_all | solution.py:54
  436.8 16.5 %reshape.79 = bf16[2560,2048]{1,0:T(8,128)(2,1)} reshape(bf16[128,1,20,2048]{3,2,1,0:T(8,128)(2,1)} %all-to-all-done.1) | data formatting | bytes 20971520 | tf_op jit(solution)/shard_map/reshape | solution.py:55
  453.2 10.1 %concatenate.3 = bf16[2561,2048]{1,0:T(8,128)(2,1)} pad(bf16[2560,2048]{1,0:T(8,128)(2,1)} %reshape.79, bf16[]{:T(256)} %constant.9.clone.1), padding=0_1x0_0 | pad | bytes 20975618 | tf_op jit(solution)/shard_map/concatenate | solution.py:56
  463.3 0.0 copy-start.1
  463.3 14.3 %gather_fusion = bf16[1024,2048]{1,0:T(8,128)(2,1)} fusion(bf16[2561,2048]{1,0:T(8,128)(2,1)} %concatenate.3, s32[1024]{0:T(1024)S(1)} %broadcast_clamp_fusion), kind=kCustom, calls=%fused_computation | custom fusion | bytes 8392704 | tf_op jit(solution)/shard_map/gather | solution.py:57
  477.6 6.5 %fusion.4 = f32[128,2048]{1,0:T(8,128)S(1)} fusion(bf16[1024,2048]{1,0:T(8,128)(2,1)} %gather_fusion, f32[128,8]{1,0:T(8,128)S(1)} %copy.20), kind=kLoop, calls=%fused_computation.8 | loop fusion | flops 6029312 | bytes 5246976 | tf_op jit(solution)/shard_map/reduce_sum | solution.py:58
  484.1 2.0 fusion.23
  486.1 0.0 copy-done.1
  (3 shorter events, 0.0 us)
Async XLA Ops:
  0.0 209.3 %copy-start = (bf16[1,768,2048]{2,1,0:T(8,128)(2,1)S(1)}, bf16[1,768,2048]{2,1,0:T(8,128)(2,1)}, u32[]{:S(2)}) copy-start(bf16[1,768,2048]{2,1,0:T(8,128)(2,1)} %param.12) | copy-start | bytes 9437188
  33.6 154.0 %copy-start.4 = (bf16[1,2048,768]{2,1,0:T(8,128)(2,1)S(1)}, bf16[1,2048,768]{2,1,0:T(8,128)(2,1)}, u32[]{:S(2)}) copy-start(bf16[1,2048,768]{2,1,0:T(8,128)(2,1)} %param.11) | copy-start | bytes 9437188
  183.0 4.5 copy-start.2
  256.5 10.1 %copy-start.3 = (f32[128,8]{0,1:T(8,128)S(1)}, f32[128,8]{0,1:T(8,128)}, u32[]{:S(2)}) copy-start(f32[128,8]{0,1:T(8,128)} %param.15) | copy-start | bytes 12292
  256.5 180.3 %all-to-all-start.1 = ((bf16[128,1,20,2048]{3,2,1,0:T(8,128)(2,1)}), bf16[128,1,20,2048]{3,2,1,0:T(8,128)(2,1)}, u32[]{:S(2)}, u32[]{:S(2)}) async-start(bf16[128,1,20,2048]{3,2,1,0:T(8,128)(2,1)} %copy.18), calls=%async_computation.1 | async-start | bytes 25165824 | tf_op jit(solution)/shard_map/all_to_all | solution.py:54
  463.3 22.8 %copy-start.1 = (bf16[1,768,2048]{2,1,0:T(8,128)(2,1)S(1)}, bf16[1,768,2048]{2,1,0:T(8,128)(2,1)}, u32[]{:S(2)}) copy-start(bf16[1,768,2048]{2,1,0:T(8,128)(2,1)} %param.12) | copy-start | bytes 9437188
where the time goes:
time: 495 us; the launch traced here: 486 us
  waiting for transfers between devices  170 us (34%)
  blocking collectives  149 us (30%)
  local copies, waits for them, and re-layouts  89.4 us (18%)
  matrix products  54.7 us (11%)
  other arithmetic  12.6 us (3%)
  starting transfers between devices  9.9 us (2%)
    all_to_all x1, waiting for transfers between devices, per_device(): lax.all_to_all(results, ('dp', 'expert'), split_axis=0, concat_axis=0, ti...  170 us
    all_to_all x1, blocking collectives, per_device(): lax.all_to_all(outgoing.reshape(token_groups, local_experts, cap_hot, wid...  149 us
    dot_general x1, matrix products, expert_work(): jnp.einsum('secf,efd->secd', hidden, w_down, preferred_element_type=jnp.f...  32.9 us
    dot_general x1, matrix products, expert_work(): jnp.einsum('secd,edf->secf', arrived, w_up, preferred_element_type=jnp.fl...  21.8 us
    reshape x1, local copies, waits for them, and re-layouts, per_device(): row_table = returned.reshape(row_count, width)  16.5 us
    reshape x1, local copies, waits for them, and re-layouts, per_device(): outgoing.reshape(token_groups, local_experts, cap_hot, width)  16.4 us
    gather x1, local copies, waits for them, and re-layouts, per_device(): picked = padded_table[row_index]  14.3 us
    convert_element_type x1, local copies, waits for them, and re-layouts, expert_work(): jnp.einsum('secf,efd->secd', hidden, w_down, preferred_element_type=jnp.f...  14.3 us
  transfers between devices with their start and end apart: 1, of which 1 were waited for; matrix products, arithmetic and copies ran while one was open for 0% of the time, Pallas kernels for 0%

commit v1 on v0

v1 whole, which is shorter than its diff:
```python
import jax
import jax.numpy as jnp
from jax import lax
from jax.experimental import pallas as pl
from jax.experimental.pallas import tpu as pltpu
from jax.sharding import PartitionSpec as P

MESH = pl.DeviceIdType.MESH
F32 = jnp.float32
BF16 = jnp.bfloat16
epsilon = 1e-06

TOK = 128
D = 2048
FF = 768
FAN = 8
CAP = 20
PAIR = 2 * CAP
WAYS = ((2, 1, 0), (0, 2, 1), (1, 0, 2))
WIDTH = (384, 384, 256)
START = (0, 384, 768)
HALF = 1024
LANES = 384
ROWS = 8 * PAIR


def my_place():
    dp = lax.axis_index("dp")
    ex = lax.axis_index("expert")
    return [(dp % 2) * 2 + ex // 2, (dp // 2) % 4, dp // 8], ex % 2


def device(place, core):
    x, y, z = place
    return (z * 8 + y * 2 + x // 2, (x % 2) * 2 + core)


def moved(place, axis, step):
    place = list(place)
    place[axis] = (place[axis] + step) % 4
    return place


def kernel(resid, gain, ids, slots, wts, wg_hbm, wu_hbm, wd_hbm, out,
           tok0, tok1, tok2, g0, g1, g2, r0, r1, r2, x0, x1, x2, a0, a1_, a2_, b0, b1, b2,
           tab, tab1, tab2s, tab2, hidden, wg, wu, wd,
           sem_w, s1s, s1r, t1s, t1r, s2s, s2r, t2s, t2r, s3s, s3r, ras, rar, rbs, rbr, rcs, rcr, q2s, q2r, q1s, q1r, free):
    place, core = my_place()
    toks, gs, rs, xs = (tok0, tok1, tok2), (g0, g1, g2), (r0, r1, r2), (x0, x1, x2)
    acc2, acc1 = (a0, a1_, a2_), (b0, b1, b2)

    def remote(src, dst, ssem, rsem, where, c):
        return pltpu.make_async_remote_copy(
            src_ref=src, dst_ref=dst, send_sem=ssem, recv_sem=rsem,
            device_id=device(where, c), device_id_type=MESH,
        )

    loads = [pltpu.make_async_copy(h, v, sem_w.at[i]) for i, (h, v) in enumerate(((wg_hbm, wg), (wu_hbm, wu), (wd_hbm, wd)))]
    for cp in loads:
        cp.start()

    barrier = pltpu.get_barrier_semaphore()
    for axis in range(3):
        for step in (1, 2, 3):
            for c in range(2):
                pl.semaphore_signal(barrier, inc=1, device_id=device(moved(place, axis, step), c), device_id_type=MESH)
    pl.semaphore_signal(barrier, inc=1, device_id=device(place, 1 - core), device_id_type=MESH)

    floats = resid[...].astype(F32)
    mean_square = jnp.mean(floats * floats, axis=1, keepdims=True)
    normed = (floats * lax.rsqrt(mean_square + epsilon) * gain[...]).astype(BF16)
    for o in range(3):
        for h in range(2):
            lo = h * HALF + START[o]
            toks[o][h] = normed[:, lo:lo + WIDTH[o]]

    pl.semaphore_wait(barrier, 19)

    def first(o, step, cc):
        one, two, _ = WAYS[o]
        h = (core + cc) % 2
        return remote(
            toks[o].at[h], gs[o].at[place[two], place[one], core],
            s1s.at[o, step, cc], s1r.at[o, step, cc], moved(place, one, step), h,
        )

    for step in (1, 3, 2, 0):
        for o in range(3):
            for cc in range(2):
                if step or cc:
                    first(o, step, cc).start()
    for o in range(3):
        one, two, _ = WAYS[o]
        gs[o][place[two], place[one], core] = toks[o][core]

    e = ids[...]
    coords = ((e >> 1) & 3, (e >> 3) & 3, e >> 5)
    sl = slots[...]
    lane = lax.broadcasted_iota(jnp.int32, (TOK, LANES), 1)
    lane128 = lax.broadcasted_iota(jnp.int32, (TOK, 128), 1)
    number = (lax.broadcasted_iota(jnp.int32, (TOK, 1), 0) + 1 + core * TOK).astype(F32)
    weight = wts[...]
    for o in range(3):
        one, two, three = WAYS[o]
        spot = jnp.where(sl >= 0, ((coords[three] * 2 + (e & 1)) * 2 + core) * CAP + sl, -1)
        line = coords[one] * 8 + coords[two]
        total = jnp.zeros((128, LANES), F32)
        for k in range(FAN):
            hit = lane == spot[:, k:k + 1]
            here = lane128 == line[:, k:k + 1]
            there = lane128 == line[:, k:k + 1] + 4
            for mask, value in ((here, number), (there, weight[:, k:k + 1])):
                total += lax.dot_general(
                    mask.astype(F32).astype(BF16), jnp.where(hit, value, 0.0).astype(BF16),
                    (((0,), (0,)), ((), ())), preferred_element_type=F32,
                )
        tab[o] = total[:32].reshape(4, 8, LANES)

    def first_table(o, step, cc):
        one, _, _ = WAYS[o]
        return remote(
            tab.at[o, (place[one] + step) % 4], tab1.at[o, place[one], core],
            t1s.at[o, step, cc], t1r.at[o, step, cc], moved(place, one, step), (core + cc) % 2,
        )

    for o in range(3):
        one, _, _ = WAYS[o]
        for step in (1, 3, 2, 0):
            for cc in range(2):
                if step or cc:
                    first_table(o, step, cc).start()
        tab1[o, place[one], core] = tab[o, place[one]]

    def second(o, step, back):
        one, two, _ = WAYS[o]
        piece = gs[o].at[place[two], (place[one] + 4 - back) % 4]
        return remote(piece, piece, s2s.at[o, step, back], s2r.at[o, step, back], moved(place, two, step), core)

    def second_table(o, step):
        two = WAYS[o][1]
        return remote(
            tab2s.at[o, (place[two] + step) % 4], tab2.at[o, place[two]],
            t2s.at[o, step], t2r.at[o, step], moved(place, two, step), core,
        )

    def first_wait(o, step, cc):
        one, two, _ = WAYS[o]
        came = gs[o].at[place[two], (place[one] + 4 - step) % 4, (core + cc) % 2]
        remote(came, came, s1s.at[o, step, cc], s1r.at[o, step, cc], place, core).wait_recv()

    def first_table_wait(o, step, cc):
        one, _, _ = WAYS[o]
        came = tab1.at[o, (place[one] + 4 - step) % 4, (core + cc) % 2]
        remote(came, came, t1s.at[o, step, cc], t1r.at[o, step, cc], place, core).wait_recv()

    for back in (0, 1, 3, 2):
        for o in range(3):
            for cc in range(2):
                if back or cc:
                    first_wait(o, back, cc)
            for step in (1, 3, 2):
                second(o, step, back).start()
    for o in range(3):
        for step in (0, 1, 3, 2):
            for cc in range(2):
                if step or cc:
                    first_table_wait(o, step, cc)
        for line in range(4):
            for a in range(4):
                tab2s[o, line, a:a + 1] = tab1[o, a, 0, line:line + 1] + tab1[o, a, 1, line:line + 1]
                tab2s[o, line, 4 + a:5 + a] = tab1[o, a, 0, 4 + line:5 + line] + tab1[o, a, 1, 4 + line:5 + line]
        for step in (1, 3, 2):
            second_table(o, step).start()
        two = WAYS[o][1]
        tab2[o, place[two]] = tab2s[o, place[two]]

    def landing(o, frm, group):
        if o == 0:
            return lambda h: xs[0].at[h, frm, group]
        if o == 1:
            return lambda h: xs[1].at[h, :, frm, group]
        return lambda h: xs[2].at[h, group, :, frm]

    def third(o, step, cc, n, group):
        three = WAYS[o][2]
        to = (place[three] + step) % 4
        c = (core + cc) % 2
        src = rs[o].at[to * 2 + c, group]
        dst = landing(o, place[three], group)(core)
        if step == 0 and cc == 0:
            return pltpu.make_async_copy(src, dst, s3r.at[o, 0, 0, n])
        return remote(src, dst, s3s.at[o, step, cc, n], s3r.at[o, step, cc, n], moved(place, three, step), c)

    def group_of(o, n):
        two = WAYS[o][1]
        gap = n ^ (n >> 1)
        return gap, (place[two] + 4 - gap) % 4

    token_lane = lax.broadcasted_iota(jnp.int32, (ROWS, 2 * TOK), 1).astype(F32) + 1.0

    def pack(n, _):
        for o in range(3):
            one, two, three = WAYS[o]
            gap, group = group_of(o, n)

            @pl.when(n > 0)
            def _():
                for back in range(4):
                    came = gs[o].at[group, (place[one] + 4 - back) % 4]
                    remote(came, came, s2s.at[o, gap, back], s2r.at[o, gap, back], place, core).wait_recv()
                came = tab2.at[o, group]
                remote(came, came, t2s.at[o, gap], t2r.at[o, gap], place, core).wait_recv()

            column = tab2[o, group].T
            for a in range(4):
                pick = jnp.where(column[:ROWS, a:a + 1] == token_lane, 1.0, 0.0).astype(BF16)
                rows = jnp.dot(pick, gs[o][group, a].reshape(2 * TOK, WIDTH[o]), preferred_element_type=F32)
                rs[o][:, group, a] = rows.astype(BF16).reshape(8, PAIR, WIDTH[o])
            for step in (1, 3, 2, 0):
                for cc in range(2):
                    third(o, step, cc, n, group).start()
        return 0

    lax.fori_loop(0, 4, pack, 0)

    for o in range(3):
        for step in range(4):
            for cc in range(2):
                if step or cc:
                    first(o, step, cc).wait_send()
                    first_table(o, step, cc).wait_send()
            if step:
                second_table(o, step).wait_send()
                for back in range(4):
                    second(o, step, back).wait_send()

    for cp in loads:
        cp.wait()

    def arrive(n, _):
        for o in range(3):
            three = WAYS[o][2]
            gap, group = group_of(o, n)
            for step in range(4):
                for cc in range(2):
                    came = landing(o, (place[three] + 4 - step) % 4, group)((core + cc) % 2)
                    if step == 0 and cc == 0:
                        third(o, 0, 0, n, group).wait()
                    else:
                        remote(came, came, s3s.at[o, step, cc, n], s3r.at[o, step, cc, n], place, core).wait_recv()
                        third(o, step, cc, n, group).wait_send()
        return 0

    lax.fori_loop(0, 4, arrive, 0)

    for o in range(3):
        for step in range(4):
            for cc in range(2):
                if step or cc:
                    pl.semaphore_signal(
                        free, inc=1, device_id=device(moved(place, WAYS[o][2], step), (core + cc) % 2), device_id_type=MESH
                    )

    mx, my, mz = place

    def send_a(s, x, q, cc, local):
        h = (core + cc) % 2
        src = xs[0].at[h, x, pl.ds(2 * q, 2)]
        dst = rs[0].at[mx * 2 + core, pl.ds(2 * q, 2)]
        if local:
            return pltpu.make_async_copy(src, dst, rar.at[s, cc])
        return remote(src, dst, ras.at[s, cc], rar.at[s, cc], (x, my, mz), h)

    def send_b(s, x, q, i, cc, local):
        h = (core + cc) % 2
        y = 2 * q + (my + i) % 2
        src = xs[1].at[h, x, y]
        dst = rs[1].at[my * 2 + core, :, x]
        if local:
            return pltpu.make_async_copy(src, dst, rbr.at[s, i, cc])
        return remote(src, dst, rbs.at[s, i, cc], rbr.at[s, i, cc], (mx, y, mz), h)

    def send_c(s, x, q, step, cc):
        h = (core + cc) % 2
        z = (mz + step) % 4
        src = xs[2].at[h, x, pl.ds(2 * q, 2), z]
        dst = rs[2].at[mz * 2 + core, x, pl.ds(2 * q, 2)]
        if step == 0 and cc == 0:
            return pltpu.make_async_copy(src, dst, rcr.at[s, 0, 0])
        return remote(src, dst, rcs.at[s, step, cc], rcr.at[s, step, cc], (mx, my, z), h)

    def block_of(s):
        return (mx + 1 + s // 2) % 4, (my // 2 + s) % 2

    def each(s, act_local, act_remote):
        x, q = block_of(s)
        for cc in range(2):
            if cc:
                act_remote(send_a(s, x, q, cc, False))
            else:
                @pl.when(s < 6)
                def _():
                    act_remote(send_a(s, x, q, 0, False))

                @pl.when(s >= 6)
                def _():
                    act_local(send_a(s, x, q, 0, True))
            for i in range(2):
                if cc or i:
                    act_remote(send_b(s, x, q, i, cc, False))
                else:
                    @pl.when(s % 2 == 1)
                    def _():
                        act_remote(send_b(s, x, q, 0, 0, False))

                    @pl.when(s % 2 == 0)
                    def _():
                        act_local(send_b(s, x, q, 0, 0, True))
            for step in (1, 3, 2, 0):
                if step == 0 and cc == 0:
                    act_local(send_c(s, x, q, 0, 0))
                else:
                    act_remote(send_c(s, x, q, step, cc))

    def expert(s, _):
        x, q = block_of(s)
        pair = pl.ds(2 * q, 2)
        parts = [xs[o][h, x, pair].reshape(ROWS, WIDTH[o]) for h in range(2) for o in range(3)]
        rows = jnp.concatenate(parts, axis=1)
        for f in range(0, FF, 256):
            gate = jnp.dot(rows, wg[:, f:f + 256], preferred_element_type=F32)
            up = jnp.dot(rows, wu[:, f:f + 256], preferred_element_type=F32)
            hidden[:, f:f + 256] = (gate / (1.0 + jnp.exp(-gate)) * up).astype(BF16)
        for h in range(2):
            for o in range(3):
                lo = h * HALF + START[o]
                res = jnp.dot(hidden[...], wd[:, lo:lo + WIDTH[o]], preferred_element_type=F32)
                xs[o][h, x, pair] = res.astype(BF16).reshape(2, 4, PAIR, WIDTH[o])

        @pl.when(s == 0)
        def _():
            pl.semaphore_wait(free, 21)

        each(s, lambda cp: cp.start(), lambda cp: cp.start())
        return 0

    lax.fori_loop(0, 8, expert, 0)

    def returned(s, _):
        each(s, lambda cp: cp.wait(), lambda cp: cp.wait())
        return 0

    lax.fori_loop(0, 8, returned, 0)

    token_row = lax.broadcasted_iota(jnp.int32, (2 * TOK, ROWS), 0).astype(F32) + 1.0

    def reduce_second(o, step):
        two = WAYS[o][1]
        return remote(
            gs[o].at[(place[two] + step) % 4], acc2[o].at[step - 1],
            q2s.at[o, step], q2r.at[o, step], moved(place, two, step), core,
        )

    for step in (1, 3, 2, 0):
        for o in range(3):
            two = WAYS[o][1]
            group = (place[two] + step) % 4
            for a in range(4):
                index = tab2[o, group, a:a + 1, :ROWS]
                w = tab2[o, group, 4 + a:5 + a, :ROWS]
                mix = jnp.where(index == token_row, w, 0.0).astype(BF16)
                part = jnp.dot(mix, rs[o][:, group, a].reshape(ROWS, WIDTH[o]), preferred_element_type=F32)
                gs[o][group, a] = part.astype(BF16).reshape(2, TOK, WIDTH[o])
            if step:
                reduce_second(o, step).start()

    def reduce_first(o, step, cc):
        one, two, _ = WAYS[o]
        c = (core + cc) % 2
        return remote(
            gs[o].at[place[two], (place[one] + step) % 4, c], acc1[o].at[step, cc],
            q1s.at[o, step, cc], q1r.at[o, step, cc], moved(place, one, step), c,
        )

    for o in range(3):
        one, two, _ = WAYS[o]
        for step in (1, 2, 3):
            reduce_second(o, step).wait()
        for step in (1, 3, 2, 0):
            a = (place[one] + step) % 4
            total = gs[o][place[two], a].astype(F32)
            for n in range(3):
                total += acc2[o][n, a].astype(F32)
            gs[o][place[two], a] = total.astype(BF16)
            for cc in range(2):
                if step or cc:
                    reduce_first(o, step, cc).start()
        acc1[o][0, 0] = gs[o][place[two], place[one], core]

    for o in range(3):
        for step in range(4):
            for cc in range(2):
                if step or cc:
                    reduce_first(o, step, cc).wait()
        for cc in range(2):
            h = (core + cc) % 2
            where = pl.ds(pl.multiple_of(h * HALF + START[o], 128), WIDTH[o])
            total = acc1[o][0, cc].astype(F32)
            for step in (1, 2, 3):
                total += acc1[o][step, cc].astype(F32)
            out[:, where] = (resid[:, where].astype(F32) + total).astype(BF16)


def per_device(resid, norm_gain, w_gate, w_up, w_down, route_ids, route_slots, route_weights):
    vmem = pl.BlockSpec(memory_space=pltpu.VMEM)
    hbm = pl.BlockSpec(memory_space=pl.ANY)

    def per_way(*lead, rows):
        return [pltpu.VMEM((*lead, rows, w), BF16) for w in WIDTH]

    dma = pltpu.SemaphoreType.DMA
    return pl.pallas_call(
        kernel,
        out_shape=jax.ShapeDtypeStruct((TOK, D), BF16),
        in_specs=[vmem] * 5 + [hbm] * 3,
        out_specs=vmem,
        scratch_shapes=[
            *per_way(2, rows=TOK),
            *per_way(4, 4, 2, rows=TOK),
            *per_way(8, 4, 4, rows=PAIR),
            *per_way(2, 4, 4, 4, rows=PAIR),
            *per_way(3, 4, 2, rows=TOK),
            *per_way(4, 2, rows=TOK),
            pltpu.VMEM((3, 4, 8, LANES), F32),
            pltpu.VMEM((3, 4, 2, 8, LANES), F32),
            pltpu.VMEM((3, 4, 8, LANES), F32),
            pltpu.VMEM((3, 4, 8, LANES), F32),
            pltpu.VMEM((ROWS, FF), BF16),
            pltpu.VMEM((D, FF), BF16),
            pltpu.VMEM((D, FF), BF16),
            pltpu.VMEM((FF, D), BF16),
            dma((3,)),
            dma((3, 4, 2)), dma((3, 4, 2)), dma((3, 4, 2)), dma((3, 4, 2)),
            dma((3, 4, 4)), dma((3, 4, 4)), dma((3, 4)), dma((3, 4)),
            dma((3, 4, 2, 4)), dma((3, 4, 2, 4)),
            dma((8, 2)), dma((8, 2)),
            dma((8, 2, 2)), dma((8, 2, 2)),
            dma((8, 4, 2)), dma((8, 4, 2)),
            dma((3, 4)), dma((3, 4)),
            dma((3, 4, 2)), dma((3, 4, 2)),
            pltpu.SemaphoreType.REGULAR,
        ],
        compiler_params=pltpu.CompilerParams(
            collective_id=0, has_side_effects=True, vmem_limit_bytes=62 * 2**20
        ),
        cost_estimate=pl.CostEstimate(flops=30 * 10**9, bytes_accessed=11 * 10**6, transcendentals=2 * 10**6),
    )(resid, norm_gain[None, :], route_ids, route_slots, route_weights, w_gate[0], w_up[0], w_down[0])


def solution(mesh):
    rows = P(("dp", "expert"), None)
    expert = P(("dp", "expert"), None, None)
    return jax.shard_map(
        per_device, mesh=mesh, in_specs=(rows, P(), expert, expert, expert, rows, rows, rows), out_specs=rows, check_vma=False
    )
```

time: 495 us -> 212 us (0.43)
  the two profiles are of different devices: /device:TPU:52 before, /device:TPU:3 now
where the time goes in v1:
time: 212 us; the launch traced here: 211 us
  Pallas kernels  205 us (97%)
  local copies, waits for them, and re-layouts  6.11 us (3%)
    pallas_call x1, Pallas kernels, per_device(): pl.pallas_call(kernel, out_shape=jax.ShapeDtypeStruct((TOK, D), BF16), in...  205 us
    unnamed x4, local copies, waits for them, and re-layouts  6.11 us

profile of v1, /device:TPU:3, one launch (start us, length us, event | category | flops | bytes accessed | tf_op | source)
XLA Modules:
  0.0 210.7 jit_solution(11087891172353742737)
XLA Ops:
  0.0 1.4 copy.9.ids
  1.4 1.4 copy.10.slots
  2.8 1.4 copy.11.wts
  4.2 204.6 %shard_map.82 = bf16[128,2048]{1,0:T(8,128)(2,1)} custom-call(bf16[128,2048]{1,0:T(8,128)(2,1)} %resid.1, f32[1,2048]{1,0:T(1,128)} %bitcast.7, s32[128,8]{1,0:T(8,128)} %copy.9.ids, s32[128,8]{1,0:T(8,128)} %copy.10.slots, f32[128,8]{1,0:T(8,128)} %copy.11.wts, bf16[2048,768]{1,0:T(8,128)(2,1)} %bitcast.4, bf16[2048,768]{1,0:T(8,128)(2,1)} %bitcast.5, ...), custom_call_target="tpu_custom_call" | custom-call | flops 30000001024 | bytes 11000000 | tf_op jit(solution)/shard_map/pallas_call | solution.py:422
  208.8 1.9 copy.13

commit v2 on v1

--- a/solution.py
+++ b/solution.py
@@ -96,25 +96,24 @@
     e = ids[...]
     coords = ((e >> 1) & 3, (e >> 3) & 3, e >> 5)
     sl = slots[...]
-    lane = lax.broadcasted_iota(jnp.int32, (TOK, LANES), 1)
-    lane128 = lax.broadcasted_iota(jnp.int32, (TOK, 128), 1)
+    lane = lax.broadcasted_iota(jnp.int32, (TOK, LANES), 1).astype(F32)
+    level = lax.broadcasted_iota(jnp.int32, (32, TOK), 0)
     number = (lax.broadcasted_iota(jnp.int32, (TOK, 1), 0) + 1 + core * TOK).astype(F32)
-    weight = wts[...]
+    weight = wts[...].T
     for o in range(3):
         one, two, three = WAYS[o]
-        spot = jnp.where(sl >= 0, ((coords[three] * 2 + (e & 1)) * 2 + core) * CAP + sl, -1)
+        spot = jnp.where(sl >= 0, ((coords[three] * 2 + (e & 1)) * 2 + core) * CAP + sl, -1).astype(F32).T
         line = coords[one] * 8 + coords[two]
-        total = jnp.zeros((128, LANES), F32)
+        total = jnp.zeros((32, LANES), F32)
         for k in range(FAN):
             hit = lane == spot[:, k:k + 1]
-            here = lane128 == line[:, k:k + 1]
-            there = lane128 == line[:, k:k + 1] + 4
+            here = level == line[k:k + 1]
+            there = level == line[k:k + 1] + 4
             for mask, value in ((here, number), (there, weight[:, k:k + 1])):
-                total += lax.dot_general(
-                    mask.astype(F32).astype(BF16), jnp.where(hit, value, 0.0).astype(BF16),
-                    (((0,), (0,)), ((), ())), preferred_element_type=F32,
+                total += jnp.dot(
+                    mask.astype(F32).astype(BF16), jnp.where(hit, value, 0.0).astype(BF16), preferred_element_type=F32
                 )
-        tab[o] = total[:32].reshape(4, 8, LANES)
+        tab[o] = total.reshape(4, 8, LANES)
 
     def first_table(o, step, cc):
         one, _, _ = WAYS[o]
@@ -136,6 +135,23 @@
         piece = gs[o].at[place[two], (place[one] + 4 - back) % 4]
         return remote(piece, piece, s2s.at[o, step, back], s2r.at[o, step, back], moved(place, two, step), core)
 
+    def forward(o, up, back):
+        one, two, _ = WAYS[o]
+        piece = gs[o].at[(place[two] + (3 if up else 1)) % 4, (place[one] + 4 - back) % 4, 0 if up else 1]
+        at = 0 if up else 2
+        return remote(piece, piece, s2s.at[o, at, back], s2r.at[o, at, back], moved(place, two, 1 if up else 3), core)
+
+    def second_wait(o, step, back):
+        one, two, _ = WAYS[o]
+        came = gs[o].at[(place[two] + 4 - step) % 4, (place[one] + 4 - back) % 4]
+        remote(came, came, s2s.at[o, step, back], s2r.at[o, step, back], place, core).wait_recv()
+
+    def forward_wait(o, up, back):
+        one, two, _ = WAYS[o]
+        at = 0 if up else 2
+        came = gs[o].at[(place[two] + 2) % 4, (place[one] + 4 - back) % 4, 0 if up else 1]
+        remote(came, came, s2s.at[o, at, back], s2r.at[o, at, back], place, core).wait_recv()
+
     def second_table(o, step):
         two = WAYS[o][1]
         return remote(
@@ -158,7 +174,7 @@
             for cc in range(2):
                 if back or cc:
                     first_wait(o, back, cc)
-            for step in (1, 3, 2):
+            for step in (1, 3):
                 second(o, step, back).start()
     for o in range(3):
         for step in (0, 1, 3, 2):
@@ -198,30 +214,42 @@
 
     token_lane = lax.broadcasted_iota(jnp.int32, (ROWS, 2 * TOK), 1).astype(F32) + 1.0
 
-    def pack(n, _):
+    def pack(o, n):
+        three = WAYS[o][2]
+        gap, group = group_of(o, n)
+        column = tab2[o, group].T
+        for a in range(4):
+            pick = jnp.where(column[:ROWS, a:a + 1] == token_lane, 1.0, 0.0).astype(BF16)
+            rows = jnp.dot(pick, gs[o][group, a].reshape(2 * TOK, WIDTH[o]), preferred_element_type=F32)
+            rs[o][:, group, a] = rows.astype(BF16).reshape(8, PAIR, WIDTH[o])
+        for step in (1, 3, 2, 0):
+            for cc in range(2):
+                third(o, step, cc, n, group).start()
+
+    for o in range(3):
+        pack(o, 0)
+    for back in (0, 1, 3, 2):
         for o in range(3):
-            one, two, three = WAYS[o]
+            for step in (1, 3):
+                second_wait(o, step, back)
+                forward(o, step == 1, back).start()
+
+    def others(n, _):
+        for o in range(3):
             gap, group = group_of(o, n)
 
-            @pl.when(n > 0)
+            @pl.when(n == 3)
             def _():
                 for back in range(4):
-                    came = gs[o].at[group, (place[one] + 4 - back) % 4]
-                    remote(came, came, s2s.at[o, gap, back], s2r.at[o, gap, back], place, core).wait_recv()
-                came = tab2.at[o, group]
-                remote(came, came, t2s.at[o, gap], t2r.at[o, gap], place, core).wait_recv()
-
-            column = tab2[o, group].T
-            for a in range(4):
-                pick = jnp.where(column[:ROWS, a:a + 1] == token_lane, 1.0, 0.0).astype(BF16)
-                rows = jnp.dot(pick, gs[o][group, a].reshape(2 * TOK, WIDTH[o]), preferred_element_type=F32)
-                rs[o][:, group, a] = rows.astype(BF16).reshape(8, PAIR, WIDTH[o])
-            for step in (1, 3, 2, 0):
-                for cc in range(2):
-                    third(o, step, cc, n, group).start()
+                    forward_wait(o, True, back)
+                    forward_wait(o, False, back)
+
+            came = tab2.at[o, group]
+            remote(came, came, t2s.at[o, gap], t2r.at[o, gap], place, core).wait_recv()
+            pack(o, n)
         return 0
 
-    lax.fori_loop(0, 4, pack, 0)
+    lax.fori_loop(1, 4, others, 0)
 
     for o in range(3):
         for step in range(4):
@@ -231,8 +259,10 @@
                     first_table(o, step, cc).wait_send()
             if step:
                 second_table(o, step).wait_send()
-                for back in range(4):
-                    second(o, step, back).wait_send()
+        for back in range(4):
+            for step in (1, 3):
+                second(o, step, back).wait_send()
+                forward(o, step == 1, back).wait_send()
 
     for cp in loads:
         cp.wait()
@@ -290,7 +320,8 @@
         return remote(src, dst, rcs.at[s, step, cc], rcr.at[s, step, cc], (mx, my, z), h)
 
     def block_of(s):
-        return (mx + 1 + s // 2) % 4, (my // 2 + s) % 2
+        turn = (s + 1) % 4
+        return (mx + (turn ^ (turn >> 1))) % 4, (my // 2 + 1 - s // 4) % 2
 
     def each(s, act_local, act_remote):
         x, q = block_of(s)
@@ -298,22 +329,22 @@
             if cc:
                 act_remote(send_a(s, x, q, cc, False))
             else:
-                @pl.when(s < 6)
+                @pl.when(s % 4 < 3)
                 def _():
                     act_remote(send_a(s, x, q, 0, False))
 
-                @pl.when(s >= 6)
+                @pl.when(s % 4 == 3)
                 def _():
                     act_local(send_a(s, x, q, 0, True))
             for i in range(2):
                 if cc or i:
                     act_remote(send_b(s, x, q, i, cc, False))
                 else:
-                    @pl.when(s % 2 == 1)
+                    @pl.when(s < 4)
                     def _():
                         act_remote(send_b(s, x, q, 0, 0, False))
 
-                    @pl.when(s % 2 == 0)
+                    @pl.when(s >= 4)
                     def _():
                         act_local(send_b(s, x, q, 0, 0, True))
             for step in (1, 3, 2, 0):
@@ -357,21 +388,40 @@
     def reduce_second(o, step):
         two = WAYS[o][1]
         return remote(
-            gs[o].at[(place[two] + step) % 4], acc2[o].at[step - 1],
+            gs[o].at[(place[two] + step) % 4], acc2[o].at[step // 2],
             q2s.at[o, step], q2r.at[o, step], moved(place, two, step), core,
         )
 
-    for step in (1, 3, 2, 0):
+    def reduce_far(o, up):
+        two = WAYS[o][1]
+        c, at = (0, 0) if up else (1, 2)
+        return remote(
+            gs[o].at[(place[two] + 2) % 4, :, c], acc2[o].at[2, :, c],
+            q2s.at[o, at], q2r.at[o, at], moved(place, two, 1 if up else 3), core,
+        )
+
+    for step in (2, 0, 1, 3):
         for o in range(3):
             two = WAYS[o][1]
             group = (place[two] + step) % 4
+            if step % 2:
+                c = step // 2
+                reduce_far(o, step == 1).wait_recv()
             for a in range(4):
                 index = tab2[o, group, a:a + 1, :ROWS]
                 w = tab2[o, group, 4 + a:5 + a, :ROWS]
                 mix = jnp.where(index == token_row, w, 0.0).astype(BF16)
                 part = jnp.dot(mix, rs[o][:, group, a].reshape(ROWS, WIDTH[o]), preferred_element_type=F32)
-                gs[o][group, a] = part.astype(BF16).reshape(2, TOK, WIDTH[o])
-            if step:
+                part = part.reshape(2, TOK, WIDTH[o])
+                if step % 2:
+                    gs[o][group, a, c] = (part[c] + acc2[o][2, a, c].astype(F32)).astype(BF16)
+                    gs[o][group, a, 1 - c] = part[1 - c].astype(BF16)
+                else:
+                    gs[o][group, a] = part.astype(BF16)
+            if step == 2:
+                reduce_far(o, True).start()
+                reduce_far(o, False).start()
+            elif step:
                 reduce_second(o, step).start()
 
     def reduce_first(o, step, cc):
@@ -384,12 +434,13 @@
 
     for o in range(3):
         one, two, _ = WAYS[o]
-        for step in (1, 2, 3):
+        for step in (1, 3):
             reduce_second(o, step).wait()
+            reduce_far(o, step == 1).wait_send()
         for step in (1, 3, 2, 0):
             a = (place[one] + step) % 4
             total = gs[o][place[two], a].astype(F32)
-            for n in range(3):
+            for n in range(2):
                 total += acc2[o][n, a].astype(F32)
             gs[o][place[two], a] = total.astype(BF16)
             for cc in range(2):
@@ -454,7 +505,7 @@
             collective_id=0, has_side_effects=True, vmem_limit_bytes=62 * 2**20
         ),
         cost_estimate=pl.CostEstimate(flops=30 * 10**9, bytes_accessed=11 * 10**6, transcendentals=2 * 10**6),
-    )(resid, norm_gain[None, :], route_ids, route_slots, route_weights, w_gate[0], w_up[0], w_down[0])
+    )(resid, norm_gain[None, :], route_ids.T, route_slots.T, route_weights.T, w_gate[0], w_up[0], w_down[0])
 
 
 def solution(mesh):

time: 212 us -> 190 us (0.90)
  Pallas kernels: 205 us -> 186 us
  local copies, waits for them, and re-layouts: 6.11 us -> 1.88 us
    pallas_call x1, Pallas kernels: 205 us -> 186 us  [per_device(): pl.pallas_call(kernel, out_shape=jax.ShapeDtypeStruct((TOK, D), BF16), in...]
    unnamed x4 -> x1, local copies, waits for them, and re-layouts: 6.11 us -> 1.88 us
where the time goes in v2:
time: 190 us; the launch traced here: 188 us
  Pallas kernels  186 us (98%)
    pallas_call x1, Pallas kernels, per_device(): pl.pallas_call(kernel, out_shape=jax.ShapeDtypeStruct((TOK, D), BF16), in...  186 us

profile of v2, /device:TPU:3, one launch (start us, length us, event | category | flops | bytes accessed | tf_op | source)
XLA Modules:
  0.0 188.3 jit_solution(11866258267114151575)
XLA Ops:
  0.0 186.4 %shard_map.82 = bf16[128,2048]{1,0:T(8,128)(2,1)} custom-call(bf16[128,2048]{1,0:T(8,128)(2,1)} %resid.1, f32[1,2048]{1,0:T(1,128)} %bitcast.10, s32[8,128]{1,0:T(8,128)} %bitcast.11, s32[8,128]{1,0:T(8,128)} %bitcast.12, f32[8,128]{1,0:T(8,128)} %bitcast.13, bf16[2048,768]{1,0:T(8,128)(2,1)} %bitcast.7, bf16[2048,768]{1,0:T(8,128)(2,1)} %bitcast.8, ...), custom_call_target="tpu_custom_call" | custom-call | flops 30000001024 | bytes 11000000 | tf_op jit(solution)/shard_map/pallas_call | solution.py:473
  186.4 1.9 copy.10
